TPU v7x, 256 devices: a whole 4x4x8 slice. The times are simulated.
256 devices in a mesh: grp: 8 (over y, z_lo), dev: 32 (over z_hi, x, core).
Axes of the slice: x: 4, y: 4, z: 8 (z_hi: 4, z_lo: 2; z = z_hi * 2 + z_lo), core: 2. Of those that a mesh axis runs over, the one named last changes fastest.
Arguments:
- reservoir: bfloat16 [262144, 1024], P(('grp', 'dev')), may hold values from -6 to 6
- send_rows: int32 [256, 8, 16], P(('grp', 'dev')), may hold values from 0 to 1023
- send_count: int32 [256, 8], P(('grp', 'dev')), may hold values from 0 to 16, as said below
- new_rows: bfloat16 [131072, 1024], P(('grp', 'dev')), may hold values from -6 to 6
- w_up: bfloat16 [1024, 2048], P('dev'), may hold values from -0.1875 to 0.1875
- w_down: bfloat16 [2048, 1024], P('dev'), may hold values from -0.125 to 0.125
- ln_gain: bfloat16 [1024], replicated, may hold values from 0.099609375 to 1.8984375
- grad_new: bfloat16 [131072, 1024], P(('grp', 'dev')), may hold values from -0.016479492 to 0.016479492
- grad_old: bfloat16 [32768, 1024], P(('grp', 'dev')), may hold values from -0.016479492 to 0.016479492
Outputs:
- block_out: bfloat16 [131072, 1024], P(('grp', 'dev'))
- grad_up: float32 [1024, 2048], P('dev')
- grad_down: float32 [2048, 1024], P('dev')
Inputs may be any that keep to these rules, and one draw needn't show every extreme that they name: send_count[s, t] slots of source s toward group t are live, the others are empty; 16 is reached in every draw, and about a quarter of the (source, group) pairs carry 8 to 16 live slots, the others 0 to 4.
All inputs are finite; a program needn't handle non-finite values.
Results may differ from a plain program's by a relative error of at most 0.024.
Values may be sent and summed in bfloat16 or wider, within the bound.
No kernel may reach another device: no remote copies, remote signals or barrier semaphores. Data moves between devices by JAX's collectives and lax.ppermute only.
A program may use at most 64 MiB of HBM per device.

v0:
```python
import jax
import jax.numpy as jnp
from jax import lax
from jax.sharding import PartitionSpec as P


def normalize(rows, ln_gain):
    values = rows.astype(jnp.float32)
    center = jnp.mean(values, axis=-1, keepdims=True)
    centred = values - center
    spread = jnp.mean(centred * centred, axis=-1, keepdims=True)
    return (centred * lax.rsqrt(spread + 1e-05) * ln_gain.astype(jnp.float32)).astype(jnp.bfloat16)


def gelu_parts(pre):
    cdf_value = 0.5 * (1.0 + lax.erf(pre * 0.7071067811865476))
    density = jnp.exp(-0.5 * pre * pre) * 0.3989422804014327
    return (pre * cdf_value, cdf_value + pre * density)


def fetch_old(picked, groups, slots, width):
    return lax.all_to_all(picked, "grp", split_axis=0, concat_axis=0, tiled=True).reshape(
        groups * slots, width
    )


def body(reservoir, send_rows, send_count, new_rows, w_up, w_down, ln_gain, grad_new, grad_old):
    groups = lax.axis_size("grp")
    slots = send_rows.shape[2]
    fresh_count = new_rows.shape[0]
    width = new_rows.shape[1]
    live = (lax.broadcasted_iota(jnp.int32, (groups, slots), 1) < send_count[0][:, None]).astype(
        jnp.bfloat16
    )
    picked = reservoir[send_rows[0].reshape(-1)].reshape(groups, slots, width) * live[:, :, None]
    up_full = lax.all_gather(w_up, "dev", axis=0, tiled=True)
    arrived = fetch_old(picked, groups, slots, width)
    normed = normalize(jnp.concatenate([new_rows, arrived], axis=0), ln_gain)
    pre = jnp.dot(normed, up_full, preferred_element_type=jnp.float32)
    act, slope = gelu_parts(pre)
    hidden = act.astype(jnp.bfloat16)
    fresh_hidden = hidden[:fresh_count]
    cot = jnp.concatenate([grad_new, grad_old], axis=0)
    mixed = jnp.dot(
        fresh_hidden,
        lax.all_gather(w_down, "dev", axis=0, tiled=True),
        preferred_element_type=jnp.float32,
    )
    back = lax.dot_general(
        cot,
        lax.all_gather(w_down, "dev", axis=0, tiled=True),
        (((1,), (1,)), ((), ())),
        preferred_element_type=jnp.float32,
    )
    block_out = (new_rows.astype(jnp.float32) + mixed).astype(jnp.bfloat16)
    pre_grad = (back * slope).astype(jnp.bfloat16)
    group_down = lax.psum_scatter(
        lax.dot_general(
            hidden, cot, (((0,), (0,)), ((), ())), preferred_element_type=jnp.float32
        ).astype(jnp.bfloat16),
        "dev",
        scatter_dimension=0,
        tiled=True,
    )
    group_up = lax.psum_scatter(
        lax.dot_general(
            normed, pre_grad, (((0,), (0,)), ((), ())), preferred_element_type=jnp.float32
        ).astype(jnp.bfloat16),
        "dev",
        scatter_dimension=0,
        tiled=True,
    )
    grad_up, grad_down = (
        lax.psum(group_up, "grp").astype(jnp.float32),
        lax.psum(group_down, "grp").astype(jnp.float32),
    )
    return (block_out, grad_up, grad_down)


def solution(mesh):
    return jax.shard_map(
        body,
        mesh=mesh,
        in_specs=(
            P(("grp", "dev"), None),
            P(("grp", "dev"), None, None),
            P(("grp", "dev"), None),
            P(("grp", "dev"), None),
            P("dev", None),
            P("dev", None),
            P(),
            P(("grp", "dev"), None),
            P(("grp", "dev"), None),
        ),
        out_specs=(P(("grp", "dev"), None), P("dev", None), P("dev", None)),
        check_vma=False,
    )
```

profile of v0, /device:TPU:2, one launch (start us, length us, event | category | flops | bytes accessed | tf_op | source)
XLA Modules:
  0.0 433.0 jit_solution(15267910627218984748)
XLA Ops:
  7.2 0.0 copy-start
  7.2 0.0 all-gather.3.cloned.1.call-start
  7.2 0.7 all-gather.3.cloned.1.call-update
  7.9 0.0 all-gather.5.cloned.1.call-start
  8.0 0.7 all-gather.5.cloned.1.call-update
  8.7 0.8 reshape_squeeze.3
  9.5 0.9 gather_fusion
  10.4 0.1 fusion.15
  10.4 0.8 broadcast_multiply_fusion
  11.2 5.8 %all-to-all-start = ((bf16[8,16,1024]{2,1,0:T(8,128)(2,1)}), bf16[8,16,1024]{2,1,0:T(8,128)(2,1)S(1)}, u32[]{:S(2)}, u32[]{:S(2)}) async-start(bf16[8,16,1024]{2,1,0:T(8,128)(2,1)} %broadcast_multiply_fusion), calls=%async_computation | async-start | bytes 524288 | tf_op jit(solution)/shard_map/all_to_all | solution.py:22
  17.0 0.0 reduce-scatter.3.cloned.1.call-start
  17.1 2.3 constant_dynamic-update-slice_fusion.1
  19.4 1.7 constant_dynamic-update-slice_fusion
  21.1 3.3 all-to-all-done
  24.3 0.2 convert_reduce_fusion
  24.6 0.5 fusion.8
  25.1 48.8 %all-gather.3.cloned.1.call-done = bf16[1024,2048]{1,0:T(8,128)(2,1)} async-done(((bf16[32,2048]{1,0:T(8,128)(2,1)}), bf16[1024,2048]{1,0:T(8,128)(2,1)}) %all-gather.3.cloned.1.call-update) | async-done | bytes 4194320 | tf_op jit(solution)/shard_map/all_gather | solution.py:36
  73.9 8.1 %multiply_convert_fusion = (bf16[640,2048]{1,0:T(8,128)(2,1)}, f32[640,2048]{1,0:T(8,128)}) fusion(bf16[1024,2048]{1,0:T(8,128)(2,1)} %all-gather.3.cloned.1.call-done, f32[1024]{0:T(1024)S(1)} %convert_element_type.43, f32[640]{0:T(1024)S(1)} %add_rsqrt_fusion, f32[640]{0:T(1024)S(1)} %broadcast_multiply_fusion.1, bf16[128,1024]{1,0:T(8,128)(2,1)S(1)} %bitcast.13, ...), kind=kOutput, calls=%fused_computation.8 | convolution fusion | flops 2696151040 | bytes 13378560 | tf_op jit(solution)/shard_map/dot_general | solution.py:39
  82.0 52.4 %all-gather.5.cloned.1.call-done = bf16[2048,1024]{1,0:T(8,128)(2,1)} async-done(((bf16[64,1024]{1,0:T(8,128)(2,1)}), bf16[2048,1024]{1,0:T(8,128)(2,1)}) %all-gather.5.cloned.1.call-update) | async-done | bytes 4194320 | tf_op jit(solution)/shard_map/all_gather | solution.py:46
  134.4 11.5 %convolution_convert_fusion.1 = bf16[1024,2048]{1,0:T(8,128)(2,1)} fusion(f32[640,2048]{1,0:T(8,128)} %get-tuple-element.6, bf16[640,1024]{1,0:T(8,128)(2,1)} %constant_dynamic-update-slice_fusion, bf16[2048,1024]{1,0:T(8,128)(2,1)} %all-gather.5.cloned.1.call-done, f32[1024]{0:T(1024)S(1)} %convert_element_type.43, f32[640]{0:T(1024)S(1)} %add_rsqrt_fusion, ...), kind=kOutput, calls=%fused_computation.11 | convolution fusion | flops 5389156352 | bytes 16262144 | tf_op jit(solution)/shard_map/dot_general | solution.py:66
  145.9 0.0 reduce-scatter.3.cloned.1.call-update
  145.9 0.0 reduce-scatter.5.cloned.1.call-start
  146.0 7.5 %convolution_convert_fusion = bf16[2048,1024]{1,0:T(8,128)(2,1)} fusion(bf16[640,2048]{1,0:T(8,128)(2,1)} %get-tuple-element.5, bf16[640,1024]{1,0:T(8,128)(2,1)} %constant_dynamic-update-slice_fusion), kind=kOutput, calls=%fused_computation.10 | convolution fusion | flops 2686451712 | bytes 8126464 | tf_op jit(solution)/shard_map/dot_general | solution.py:58
  153.5 0.0 reduce-scatter.5.cloned.1.call-update
  153.5 0.0 all-reduce.3.cloned.1.call-start
  153.6 88.5 %reduce-scatter.3.cloned.1.call-done = bf16[32,2048]{1,0:T(8,128)(2,1)} async-done(((bf16[1024,2048]{1,0:T(8,128)(2,1)}), bf16[32,2048]{1,0:T(8,128)(2,1)}) %reduce-scatter.3.cloned.1.call-update) | async-done | bytes 131088 | tf_op jit(solution)/shard_map/reduce_scatter | solution.py:65
  242.1 101.2 %reduce-scatter.5.cloned.1.call-done = bf16[64,1024]{1,0:T(8,128)(2,1)} async-done(((bf16[2048,1024]{1,0:T(8,128)(2,1)}), bf16[64,1024]{1,0:T(8,128)(2,1)}) %reduce-scatter.5.cloned.1.call-update) | async-done | bytes 131088 | tf_op jit(solution)/shard_map/reduce_scatter | solution.py:57
  343.3 0.0 all-reduce.3.cloned.1.call-update
  343.4 6.1 %add_convert_fusion = bf16[512,1024]{1,0:T(8,128)(2,1)} fusion(bf16[512,1024]{1,0:T(8,128)(2,1)S(1)} %copy-done.1, bf16[2048,1024]{1,0:T(8,128)(2,1)} %all-gather.5.cloned.1.call-done, bf16[640,2048]{1,0:T(8,128)(2,1)} %get-tuple-element.5), kind=kOutput, calls=%fused_computation.21 | convolution fusion | flops 2149056512 | bytes 8388608 | tf_op jit(solution)/shard_map/dot_general | solution.py:44
  349.5 73.7 %all-reduce.3.cloned.1.call-done = (bf16[32,2048]{1,0:T(8,128)(2,1)}, bf16[64,1024]{1,0:T(8,128)(2,1)}) async-done(((bf16[32,2048]{1,0:T(8,128)(2,1)}, bf16[64,1024]{1,0:T(8,128)(2,1)}), (bf16[32,2048]{1,0:T(8,128)(2,1)}, bf16[64,1024]{1,0:T(8,128)(2,1)})) %all-reduce.3.cloned.1.call-update) | async-done | bytes 262160 | tf_op jit(solution)/shard_map/psum | solution.py:74
  423.2 1.6 convert_element_type.49
  424.8 1.6 convert_element_type.51
  (12 shorter events, 0.0 us)
Async XLA Ops:
  7.2 2.3 copy-start
  7.2 3.2 copy-start.3
  7.2 9.9 %copy-start.2 = (bf16[1024]{0:T(1024)(128)(2,1)S(1)}, bf16[1024]{0:T(1024)(128)(2,1)}, u32[]{:S(2)}) copy-start(bf16[1024]{0:T(1024)(128)(2,1)} %param.15) | copy-start | bytes 6148
  7.2 66.7 %all-gather.3.cloned.1.call-start = ((), (), s32[]{:S(2)}) async-start(), calls=%async_computation.3 | async-start | bytes 4325376 | tf_op jit(solution)/shard_map/all_gather | solution.py:36
  7.9 126.5 %all-gather.5.cloned.1.call-start = ((), (), s32[]{:S(2)}) async-start(), calls=%async_computation.4 | async-start | bytes 4325376 | tf_op jit(solution)/shard_map/all_gather | solution.py:46
  9.5 14.9 %copy-start.1 = (bf16[512,1024]{1,0:T(8,128)(2,1)S(1)}, bf16[512,1024]{1,0:T(8,128)(2,1)}, u32[]{:S(2)}) copy-start(bf16[512,1024]{1,0:T(8,128)(2,1)} %param.12) | copy-start | bytes 3145732
  11.2 13.1 %all-to-all-start = ((bf16[8,16,1024]{2,1,0:T(8,128)(2,1)}), bf16[8,16,1024]{2,1,0:T(8,128)(2,1)S(1)}, u32[]{:S(2)}, u32[]{:S(2)}) async-start(bf16[8,16,1024]{2,1,0:T(8,128)(2,1)} %broadcast_multiply_fusion), calls=%async_computation | async-start | bytes 524288 | tf_op jit(solution)/shard_map/all_to_all | solution.py:22
  17.0 225.0 %reduce-scatter.3.cloned.1.call-start = ((), (), s32[]{:S(2)}) async-start(), calls=%async_computation.5 | async-start | bytes 4325376 | tf_op jit(solution)/shard_map/reduce_scatter | solution.py:65
  145.9 197.4 %reduce-scatter.5.cloned.1.call-start = ((), (), s32[]{:S(2)}) async-start(), calls=%async_computation.6 | async-start | bytes 4325376 | tf_op jit(solution)/shard_map/reduce_scatter | solution.py:57
  153.5 269.7 %all-reduce.3.cloned.1.call-start = ((), (), s32[]{:S(2)}) async-start(), calls=%async_computation.7 | async-start | bytes 524288 | tf_op jit(solution)/shard_map/psum | solution.py:74
Sparse Core Ops, SparseCore 0:
  10.6 63.2 all-gather.2
  76.4 57.8 all-gather.4
  146.0 96.0 reduce-scatter.2
  246.4 96.8 reduce-scatter.4
  345.8 77.3 all-reduce.2
where the time goes:
time: 433 us
  waiting for transfers between devices  369 us (85%)
  matrix products  33.3 us (8%)
  between operations  13.9 us (3%)
  starting transfers between devices  6.02 us (1%)
  local copies, waits for them, and re-layouts  5.59 us (1%)
  other arithmetic  4.86 us (1%)
    reduce_scatter x1, waiting for transfers between devices, body(): lax.psum_scatter(lax.dot_general(hidden, cot, (((0,), (0,)), ((), ())), p...  101 us
    reduce_scatter x1, waiting for transfers between devices, body(): lax.psum_scatter(lax.dot_general(normed, pre_grad, (((0,), (0,)), ((), ()...  88.5 us
    psum x1, waiting for transfers between devices, body(): lax.psum(group_up, 'grp').astype(jnp.float32)  73.7 us
    all_gather x1, waiting for transfers between devices, body(): lax.all_gather(w_down, 'dev', axis=0, tiled=True)  52.4 us
    all_gather x1, waiting for transfers between devices, body(): up_full = lax.all_gather(w_up, 'dev', axis=0, tiled=True)  48.8 us
    dot_general x1, matrix products, body(): lax.dot_general(normed, pre_grad, (((0,), (0,)), ((), ())), preferred_ele...  11.5 us
  transfers between devices with their start and end apart: 6, of which 6 were waited for; matrix products, arithmetic and copies ran while one was open for 7% of the time, Pallas kernels for 0%

commit v1 on v0

--- a/solution.py
+++ b/solution.py
@@ -71,7 +71,7 @@
         tiled=True,
     )
     grad_up, grad_down = (
-        lax.psum(group_up, "grp").astype(jnp.float32),
+        jnp.sum(lax.all_gather(group_up, "grp"), axis=0).astype(jnp.float32),
         lax.psum(group_down, "grp").astype(jnp.float32),
     )
     return (block_out, grad_up, grad_down)

time: 433 us -> 467 us (1.079)
  waiting for transfers between devices: 369 us -> 403 us
    all_gather x0 -> x1, waiting for transfers between devices: none -> 41.9 us  [body(): lax.all_gather(group_up, 'grp')]
    reduce_scatter x1, waiting for transfers between devices: 101 us -> 88.5 us  [body(): lax.psum_scatter(lax.dot_general(hidden, cot, (((0,), (0,)), ((), ())), p...]
    reduce_scatter x1, waiting for transfers between devices: 88.5 us -> 101 us  [body(): lax.psum_scatter(lax.dot_general(normed, pre_grad, (((0,), (0,)), ((), ()...]
    all_gather x1, waiting for transfers between devices: 52.4 us -> 45 us  [body(): lax.all_gather(w_down, 'dev', axis=0, tiled=True)]
  transfers between devices with their start and end apart: 6 -> 7, of which waited for: 6 -> 7; matrix products, arithmetic and copies ran while one was open for 7% -> 9% of each run, Pallas kernels for 0% -> 0%
where the time goes in v1:
time: 467 us
  waiting for transfers between devices  403 us (86%)
  matrix products  31.6 us (7%)
  between operations  14.2 us (3%)
  local copies, waits for them, and re-layouts  7.12 us (2%)
  starting transfers between devices  6.06 us (1%)
  other arithmetic  5.34 us (1%)
    reduce_scatter x1, waiting for transfers between devices, body(): lax.psum_scatter(lax.dot_general(normed, pre_grad, (((0,), (0,)), ((), ()...  101 us
    reduce_scatter x1, waiting for transfers between devices, body(): lax.psum_scatter(lax.dot_general(hidden, cot, (((0,), (0,)), ((), ())), p...  88.5 us
    psum x1, waiting for transfers between devices, body(): lax.psum(group_down, 'grp').astype(jnp.float32)  72.6 us
    all_gather x1, waiting for transfers between devices, body(): up_full = lax.all_gather(w_up, 'dev', axis=0, tiled=True)  48.8 us
    all_gather x1, waiting for transfers between devices, body(): lax.all_gather(w_down, 'dev', axis=0, tiled=True)  45 us
    all_gather x1, waiting for transfers between devices, body(): lax.all_gather(group_up, 'grp')  41.9 us
    dot_general x1, matrix products, body(): lax.dot_general(normed, pre_grad, (((0,), (0,)), ((), ())), preferred_ele...  11.4 us
  transfers between devices with their start and end apart: 7, of which 7 were waited for; matrix products, arithmetic and copies ran while one was open for 9% of the time, Pallas kernels for 0%

profile of v1, /device:TPU:2, one launch (start us, length us, event | category | flops | bytes accessed | tf_op | source)
XLA Modules:
  0.0 466.9 jit_solution(15349249381747992614)
XLA Ops:
  7.2 0.0 all-gather.5.cloned.1.call-start
  7.2 0.7 all-gather.5.cloned.1.call-update
  7.9 0.0 all-gather.7.cloned.1.call-start
  8.0 0.7 all-gather.7.cloned.1.call-update
  8.7 0.8 reshape_squeeze.3
  9.5 0.9 gather_fusion
  10.4 0.1 fusion.15
  10.4 0.8 broadcast_multiply_fusion
  11.2 5.8 %all-to-all-start = ((bf16[8,16,1024]{2,1,0:T(8,128)(2,1)}), bf16[8,16,1024]{2,1,0:T(8,128)(2,1)S(1)}, u32[]{:S(2)}, u32[]{:S(2)}) async-start(bf16[8,16,1024]{2,1,0:T(8,128)(2,1)} %broadcast_multiply_fusion), calls=%async_computation | async-start | bytes 524288 | tf_op jit(solution)/shard_map/all_to_all | solution.py:22
  17.0 0.0 reduce-scatter.5.cloned.1.call-start
  17.1 2.3 constant_dynamic-update-slice_fusion.1
  19.4 1.7 constant_dynamic-update-slice_fusion
  21.1 3.2 all-to-all-done
  24.3 0.2 convert_reduce_fusion
  24.6 0.5 fusion.8
  25.1 48.8 %all-gather.5.cloned.1.call-done = bf16[1024,2048]{1,0:T(8,128)(2,1)} async-done(((bf16[32,2048]{1,0:T(8,128)(2,1)}), bf16[1024,2048]{1,0:T(8,128)(2,1)}) %all-gather.5.cloned.1.call-update) | async-done | bytes 4194320 | tf_op jit(solution)/shard_map/all_gather | solution.py:36
  73.9 7.7 %multiply_convert_fusion = (bf16[640,2048]{1,0:T(8,128)(2,1)S(1)}, f32[640,2048]{1,0:T(8,128)}) fusion(bf16[1024,2048]{1,0:T(8,128)(2,1)} %all-gather.5.cloned.1.call-done, f32[1024]{0:T(1024)S(1)} %convert_element_type.45, f32[640]{0:T(1024)S(1)} %add_rsqrt_fusion, f32[640]{0:T(1024)S(1)} %broadcast_multiply_fusion.1, bf16[128,1024]{1,0:T(8,128)(2,1)S(1)} %bitcast.14, ...), kind=kOutput, calls=%fused_computation.8 | convolution fusion | flops 2696151040 | bytes 13378560 | tf_op jit(solution)/shard_map/dot_general | solution.py:39
  81.6 1.5 copy-done.4
  83.1 6.3 %convolution_convert_fusion = bf16[2048,1024]{1,0:T(8,128)(2,1)} fusion(bf16[640,2048]{1,0:T(8,128)(2,1)S(1)} %get-tuple-element.3, bf16[640,1024]{1,0:T(8,128)(2,1)} %constant_dynamic-update-slice_fusion), kind=kOutput, calls=%fused_computation.10 | convolution fusion | flops 2686451712 | bytes 8126464 | tf_op jit(solution)/shard_map/dot_general | solution.py:58
  89.4 0.0 reduce-scatter.3.cloned.1.call-start
  89.4 45.0 %all-gather.7.cloned.1.call-done = bf16[2048,1024]{1,0:T(8,128)(2,1)} async-done(((bf16[64,1024]{1,0:T(8,128)(2,1)}), bf16[2048,1024]{1,0:T(8,128)(2,1)}) %all-gather.7.cloned.1.call-update) | async-done | bytes 4194320 | tf_op jit(solution)/shard_map/all_gather | solution.py:46
  134.4 11.4 %convolution_convert_fusion.1 = bf16[1024,2048]{1,0:T(8,128)(2,1)} fusion(f32[640,2048]{1,0:T(8,128)} %get-tuple-element.4, bf16[640,1024]{1,0:T(8,128)(2,1)} %constant_dynamic-update-slice_fusion, bf16[2048,1024]{1,0:T(8,128)(2,1)} %all-gather.7.cloned.1.call-done, f32[1024]{0:T(1024)S(1)} %convert_element_type.45, f32[640]{0:T(1024)S(1)} %add_rsqrt_fusion, ...), kind=kOutput, calls=%fused_computation.11 | convolution fusion | flops 5389156352 | bytes 16262144 | tf_op jit(solution)/shard_map/dot_general | solution.py:66
  145.9 0.0 all-reduce.2.cloned.1.call-start
  145.9 88.5 %reduce-scatter.5.cloned.1.call-done = bf16[64,1024]{1,0:T(8,128)(2,1)} async-done(((bf16[2048,1024]{1,0:T(8,128)(2,1)}), bf16[64,1024]{1,0:T(8,128)(2,1)}) %reduce-scatter.5.cloned.1.call-update) | async-done | bytes 131088 | tf_op jit(solution)/shard_map/reduce_scatter | solution.py:57
  234.5 0.0 all-gather.9.cloned.1.call-start
  234.5 101.2 %reduce-scatter.3.cloned.1.call-done = bf16[32,2048]{1,0:T(8,128)(2,1)} async-done(((bf16[1024,2048]{1,0:T(8,128)(2,1)}), bf16[32,2048]{1,0:T(8,128)(2,1)}) %reduce-scatter.3.cloned.1.call-update) | async-done | bytes 131088 | tf_op jit(solution)/shard_map/reduce_scatter | solution.py:65
  335.7 6.1 %add_convert_fusion = bf16[512,1024]{1,0:T(8,128)(2,1)} fusion(bf16[512,1024]{1,0:T(8,128)(2,1)S(1)} %copy-done.1, bf16[2048,1024]{1,0:T(8,128)(2,1)} %all-gather.7.cloned.1.call-done, bf16[640,2048]{1,0:T(8,128)(2,1)} %copy-done.4), kind=kOutput, calls=%fused_computation.21 | convolution fusion | flops 2149056512 | bytes 8388608 | tf_op jit(solution)/shard_map/dot_general | solution.py:44
  341.9 72.6 %all-reduce.2.cloned.1.call-done = bf16[64,1024]{1,0:T(8,128)(2,1)} async-done(((bf16[64,1024]{1,0:T(8,128)(2,1)}), bf16[64,1024]{1,0:T(8,128)(2,1)}) %all-reduce.2.cloned.1.call-update) | async-done | bytes 131088 | tf_op jit(solution)/shard_map/psum | solution.py:75
  414.5 1.6 convert_element_type.53
  416.1 41.9 %all-gather.9.cloned.1.call-done = bf16[256,2048]{1,0:T(8,128)(2,1)} async-done(((bf16[32,2048]{1,0:T(8,128)(2,1)}), bf16[256,2048]{1,0:T(8,128)(2,1)}) %all-gather.9.cloned.1.call-update) | async-done | bytes 1048592 | tf_op jit(solution)/shard_map/all_gather | solution.py:74
  458.0 1.4 reduce_sum.32
  459.4 0.7 convert_element_type.51
  (18 shorter events, 0.1 us)
Async XLA Ops:
  7.2 2.3 copy-start
  7.2 3.2 copy-start.3
  7.2 9.9 %copy-start.2 = (bf16[1024]{0:T(1024)(128)(2,1)S(1)}, bf16[1024]{0:T(1024)(128)(2,1)}, u32[]{:S(2)}) copy-start(bf16[1024]{0:T(1024)(128)(2,1)} %param.15) | copy-start | bytes 6148
  7.2 66.7 %all-gather.5.cloned.1.call-start = ((), (), s32[]{:S(2)}) async-start(), calls=%async_computation.3 | async-start | bytes 4325376 | tf_op jit(solution)/shard_map/all_gather | solution.py:36
  7.9 126.5 %all-gather.7.cloned.1.call-start = ((), (), s32[]{:S(2)}) async-start(), calls=%async_computation.4 | async-start | bytes 4325376 | tf_op jit(solution)/shard_map/all_gather | solution.py:46
  9.5 14.9 %copy-start.1 = (bf16[512,1024]{1,0:T(8,128)(2,1)S(1)}, bf16[512,1024]{1,0:T(8,128)(2,1)}, u32[]{:S(2)}) copy-start(bf16[512,1024]{1,0:T(8,128)(2,1)} %param.12) | copy-start | bytes 3145732
  11.2 13.1 %all-to-all-start = ((bf16[8,16,1024]{2,1,0:T(8,128)(2,1)}), bf16[8,16,1024]{2,1,0:T(8,128)(2,1)S(1)}, u32[]{:S(2)}, u32[]{:S(2)}) async-start(bf16[8,16,1024]{2,1,0:T(8,128)(2,1)} %broadcast_multiply_fusion), calls=%async_computation | async-start | bytes 524288 | tf_op jit(solution)/shard_map/all_to_all | solution.py:22
  17.0 217.4 %reduce-scatter.5.cloned.1.call-start = ((), (), s32[]{:S(2)}) async-start(), calls=%async_computation.6 | async-start | bytes 4325376 | tf_op jit(solution)/shard_map/reduce_scatter | solution.py:57
  81.6 1.5 copy-start.4
  89.4 246.3 %reduce-scatter.3.cloned.1.call-start = ((), (), s32[]{:S(2)}) async-start(), calls=%async_computation.5 | async-start | bytes 4325376 | tf_op jit(solution)/shard_map/reduce_scatter | solution.py:65
  145.9 268.6 %all-reduce.2.cloned.1.call-start = ((), (), s32[]{:S(2)}) async-start(), calls=%async_computation.7 | async-start | bytes 262144 | tf_op jit(solution)/shard_map/psum | solution.py:75
  234.5 223.5 %all-gather.9.cloned.1.call-start = ((), (), s32[]{:S(2)}) async-start(), calls=%async_computation.8 | async-start | bytes 1179648 | tf_op jit(solution)/shard_map/all_gather | solution.py:74
Sparse Core Ops, SparseCore 0:
  10.6 63.2 all-gather.4
  76.4 57.8 all-gather.6
  138.3 96.0 reduce-scatter.4
  238.8 96.9 reduce-scatter.2
  338.2 76.2 all-reduce.1
  416.3 41.6 all-gather.8
